TPU v7x, 512 devices: a whole 4x8x8 slice. The times are simulated.
512 devices in a mesh: ctx: 32 (over x, y), tp: 16 (over z, core).
Axes of the slice: x: 4, y: 8, z: 8, core: 2. Of those that a mesh axis runs over, the one named last changes fastest.
Arguments:
- prefix_x: bfloat16 [8192, 8192], P('ctx', 'tp'), may hold values from -6 to 6
- prefix_z: bfloat16 [8192, 8192], P('ctx', 'tp'), may hold values from -6 to 6
- prefix_bc: bfloat16 [8192, 256], P(('ctx', 'tp')), may hold values from -6 to 6
- prefix_dt: float32 [128, 8192], P('tp', 'ctx'), may hold values from -6 to 6
- branch_x: bfloat16 [8192, 8192], P('ctx', 'tp'), may hold values from -6 to 6
- branch_z: bfloat16 [8192, 8192], P('ctx', 'tp'), may hold values from -6 to 6
- branch_bc: bfloat16 [8192, 256], P(('ctx', 'tp')), may hold values from -6 to 6
- branch_dt: float32 [128, 8192], P('tp', 'ctx'), may hold values from -6 to 6
- conv_x: bfloat16 [4, 8192], P(None, 'tp'), may hold values from -3 to 3
- conv_bc: bfloat16 [4, 256], replicated, may hold values from -3 to 3
- decay_rate: float32 [128], P('tp'), may hold values from 2.4414063e-05 to 0.03
- skip: float32 [128], P('tp'), may hold values from 0.5 to 1.5
- norm_gain: float32 [8192], P('tp'), may hold values from 0.5 to 1.5
- bound_pos: int32 [8], replicated, may hold values from 0 to 8191
- branch_owner: int32 [64], replicated, may hold values from 0 to 31, as said below
- branch_parent: int32 [64], replicated, may hold values from 0 to 7
- branch_len: int32 [64], replicated, may hold values from 1 to 255, as said below
Outputs:
- prefix_out: bfloat16 [8192, 8192], P('ctx', 'tp')
- branch_out: bfloat16 [8192, 8192], P('ctx', 'tp')
Inputs may be any that keep to these rules, and one draw needn't show every extreme that they name: `branch_owner`: every block index 0 to 31 holds exactly 2 branches. `branch_len`: the branches of one block have lengths that sum to at most 256; in every draw some block's sum is exactly 256, and some branch has exactly 255 rows.
All inputs are finite; a program needn't handle non-finite values.
Results may differ from a plain program's by a relative error of at most 0.0034.
Values may be sent and summed in bfloat16 or wider, within the bound.
No kernel may reach another device: no remote copies, remote signals or barrier semaphores. Data moves between devices by JAX's collectives and lax.ppermute only.
A program may use at most 64 MiB of HBM per device.

v0:
```python
import jax
import jax.numpy as jnp
from jax import lax
from jax.sharding import PartitionSpec as P

BR_PER = 2
EPSILON = 1e-05
SLOTS = 8
BF = jnp.bfloat16
F32 = jnp.float32
HIGH = lax.Precision.HIGHEST


def conv_silu(lagged, weights):
    summed = weights[0].astype(F32)[None, :] * lagged[0].astype(F32)
    for tap in range(1, len(lagged)):
        summed = summed + weights[tap].astype(F32)[None, :] * lagged[tap].astype(F32)
    return jax.nn.silu(summed).astype(BF)


def split_conv(convolved, channels, heads):
    length = convolved.shape[0]
    state = (convolved.shape[1] - channels) // 2
    values = convolved[:, :channels].reshape(length, heads, channels // heads)
    return (values, convolved[:, channels : channels + state], convolved[:, channels + state :])


def decays(raw_steps, rates):
    length = raw_steps.shape[1]
    step = jax.nn.softplus(raw_steps)
    log_decay = -rates[:, None] * step
    index = jnp.arange(length, dtype=jnp.int32)
    upper = (index[:, None] <= index[None, :]).astype(F32)
    return (step, log_decay, jnp.dot(log_decay, upper, precision=HIGH))


def intra(values, b_rows, c_rows, step, cumulative, mask):
    scores = jnp.dot(c_rows, b_rows.T, preferred_element_type=F32)
    exponent = jnp.where(mask[None], cumulative[:, :, None] - cumulative[:, None, :], 0.0)
    mixing = jnp.where(mask[None], scores[None] * jnp.exp(exponent) * step[:, None, :], 0.0)
    return jnp.einsum("hts,shp->thp", mixing.astype(BF), values, preferred_element_type=F32)


def pick(array, positions):
    index = jnp.arange(array.shape[1], dtype=jnp.int32)
    hit = index[None, None, :] == positions[:, None, None]
    return jnp.sum(jnp.where(hit, array[None], 0.0), axis=2)


def local_states(values, b_rows, step, cumulative, positions):
    length = cumulative.shape[1]
    ends = pick(cumulative, positions)
    row = jnp.arange(length, dtype=jnp.int32)
    inside = (row[None, :] <= positions[:, None])[:, None, :]
    exponent = jnp.where(inside, ends[:, :, None] - cumulative[None], 0.0)
    weight = jnp.where(inside, jnp.exp(exponent) * step[None], 0.0)
    weighted = (jnp.transpose(weight, (0, 2, 1))[:, :, :, None] * values[None].astype(F32)).astype(
        BF
    )
    states = jnp.einsum("jshp,sn->jhpn", weighted, b_rows, preferred_element_type=F32)
    return (states, ends)


def from_state(c_rows, state, weight):
    result = jnp.einsum("tn,hpn->thp", c_rows, state, preferred_element_type=F32)
    return result * weight.T[:, :, None]


def parts_of(value, count):
    found = []
    for _ in range(count):
        part = lax.reduce_precision(value, 8, 7)
        found.append(part.astype(BF))
        value = value - part
    return found


def body(
    prefix_x,
    prefix_z,
    prefix_bc,
    prefix_dt,
    branch_x,
    branch_z,
    branch_bc,
    branch_dt,
    conv_x,
    conv_bc,
    decay_rate,
    skip,
    norm_gain,
    bound_pos,
    branch_owner,
    branch_parent,
    branch_len,
):
    n_ctx = lax.axis_size("ctx")
    me = lax.axis_index("ctx")
    length, channels = prefix_x.shape
    heads = decay_rate.shape[0]
    width = prefix_bc.shape[1]
    n_state = width // 2
    bounds = bound_pos.shape[0]
    branches = branch_owner.shape[0]
    weights = jnp.concatenate([conv_x, conv_bc], axis=1)
    taps = weights.shape[0]
    tail = taps - 1
    row_width = channels + width
    gathered = lax.all_gather(
        jnp.concatenate([prefix_bc, branch_bc], axis=1), "tp", axis=0, tiled=True
    )
    joined = jnp.concatenate([prefix_x, gathered[:, :width]], axis=1)
    before = lax.ppermute(joined[length - tail :], "ctx", [(i, i + 1) for i in range(n_ctx - 1)])
    extended = jnp.concatenate([before, joined], axis=0)
    lagged = [extended[tap : tap + length] for tap in range(taps)]
    values, b_rows, c_rows = split_conv(conv_silu(lagged, weights), channels, heads)
    step, _, cumulative = decays(prefix_dt, decay_rate)
    block_of = bound_pos // length
    at = bound_pos - block_of * length
    order = jnp.arange(bounds, dtype=jnp.int32)
    slot_of = jnp.sum(
        ((block_of[:, None] == block_of[None, :]) & (order[None, :] < order[:, None])).astype(
            jnp.int32
        ),
        axis=1,
    )
    border = jnp.arange(branches, dtype=jnp.int32)
    same = branch_owner[:, None] == branch_owner[None, :]
    earlier = same & (border[None, :] < border[:, None])
    rank = jnp.sum(earlier.astype(jnp.int32), axis=1)
    start = jnp.sum(jnp.where(earlier, branch_len[None, :], 0), axis=1)
    place = jnp.arange(n_ctx * BR_PER, dtype=jnp.int32)
    chosen = place[:, None] == (branch_owner * BR_PER + rank)[None, :]
    parent_of = jnp.sum(jnp.where(chosen, branch_parent[None, :], 0), axis=1)
    mine = (me * BR_PER + jnp.arange(BR_PER, dtype=jnp.int32))[:, None] == (
        branch_owner * BR_PER + rank
    )[None, :]
    my_len = jnp.sum(jnp.where(mine, branch_len[None, :], 0), axis=1)
    my_start = jnp.sum(jnp.where(mine, start[None, :], 0), axis=1)
    slot_here = (block_of == me)[None, :] & (
        slot_of[None, :] == jnp.arange(SLOTS, dtype=jnp.int32)[:, None]
    )
    positions = jnp.sum(jnp.where(slot_here, at[None, :] + 1, 0), axis=1) - 1
    positions = jnp.concatenate([jnp.full((1,), length - 1, jnp.int32), positions])
    states, ends = local_states(values, b_rows, step, cumulative, positions)
    slices = states.reshape(SLOTS + 1, n_ctx, -1, n_state)
    rows = slices.shape[2]
    end_hi, end_lo = parts_of(slices[0], 2)
    partial = jnp.transpose(slices[1:].astype(BF), (1, 0, 2, 3)).reshape(
        n_ctx, SLOTS * rows, n_state
    )
    per_head = jnp.repeat(
        jnp.pad(ends.T, ((0, 0), (0, n_state - SLOTS - 1))), n_ctx // heads, axis=0
    )
    logs = jnp.stack(parts_of(per_head, 3), axis=1)
    parent_hit = parent_of[:, None] == order[None, :]
    parent_at = jnp.sum(jnp.where(parent_hit, at[None, :], 0), axis=1)
    parent_block = jnp.sum(jnp.where(parent_hit, block_of[None, :], 0), axis=1)
    wanted = parent_at[:, None] + 1 + jnp.arange(tail, dtype=jnp.int32)[None, :]
    wanted = jnp.where((parent_block == me)[:, None], wanted, -1).reshape(-1)
    picker = (wanted[:, None] == jnp.arange(length + tail, dtype=jnp.int32)[None, :]).astype(BF)
    tails = jnp.dot(picker, extended, preferred_element_type=F32).astype(BF)
    tails = tails.reshape(n_ctx, BR_PER * tail * row_width // n_state, n_state)
    pieces = [end_hi, end_lo, partial, tails, logs]
    sent = jnp.concatenate(pieces, axis=1)
    sent = jnp.pad(sent, ((0, 0), (0, -sent.shape[1] % 16), (0, 0)))
    got = lax.all_to_all(sent, "ctx", 0, 0, tiled=True)
    edges = [0]
    for piece in pieces:
        edges.append(edges[-1] + piece.shape[1])
    end_hi, end_lo, partial, tails, logs = [
        got[:, first:last].astype(F32) for first, last in zip(edges[:-1], edges[1:], strict=True)
    ]
    ends = jnp.sum(logs, axis=1)[:, : SLOTS + 1]
    block = jnp.arange(n_ctx, dtype=jnp.int32)
    totals = jnp.sum(jnp.where(block[None, :] <= block[:, None], ends[:, 0][None, :], 0.0), axis=1)
    gap = (totals - ends[:, 0])[:, None] - totals[None, :]
    earlier_block = block[None, :] < block[:, None]
    carry = jnp.where(earlier_block, jnp.exp(jnp.where(earlier_block, gap, 0.0)), 0.0)
    entering = jnp.dot(carry, (end_hi + end_lo).reshape(n_ctx, -1), precision=HIGH)
    held = block[None, :] == block_of[:, None]
    bound_end = jnp.sum(
        jnp.where(
            held[:, :, None]
            & (slot_of[:, None, None] == jnp.arange(SLOTS, dtype=jnp.int32)[None, None, :]),
            ends[None, :, 1:],
            0.0,
        ),
        axis=(1, 2),
    )
    choose = jnp.where(held, jnp.exp(bound_end)[:, None], 0.0)
    slot_pick = (
        held[:, :, None]
        & (slot_of[:, None, None] == jnp.arange(SLOTS, dtype=jnp.int32)[None, None, :])
    ).reshape(bounds, -1)
    bound_state = jnp.dot(choose, entering, precision=HIGH) + jnp.dot(
        slot_pick.astype(BF),
        partial.astype(BF).reshape(n_ctx * SLOTS, -1),
        preferred_element_type=F32,
    )
    seeds = jnp.dot(parent_hit.astype(F32), bound_state, precision=HIGH).reshape(
        n_ctx, BR_PER * rows, n_state
    )
    back = jnp.concatenate([entering.reshape(n_ctx, rows, n_state), seeds], axis=1).astype(BF)
    back = lax.all_to_all(back, "ctx", 0, 0, tiled=True)
    row = jnp.arange(length, dtype=jnp.int32)
    mixed = intra(values, b_rows, c_rows, step, cumulative, row[None, :] <= row[:, None])
    inside = (row[None, :] >= my_start[:, None]) & (row[None, :] < (my_start + my_len)[:, None])
    live = inside[0] | inside[1]
    segment = jnp.where(inside[0], 0, jnp.where(inside[1], 1, BR_PER))
    offset = row - jnp.sum(jnp.where(inside, my_start[:, None], 0), axis=0)
    tail_rows = jnp.sum(tails, axis=0).astype(BF).reshape(BR_PER * tail, row_width)
    branch_joined = jnp.concatenate([branch_x, gathered[:, width:]], axis=1)
    column = jnp.arange(BR_PER * tail, dtype=jnp.int32)
    lagged = []
    for shift in range(tail, 0, -1):
        shifted = jnp.concatenate(
            [jnp.zeros((shift, row_width), BF), branch_joined[: length - shift]], axis=0
        )
        local = jnp.where((offset >= shift)[:, None], shifted, jnp.zeros_like(shifted))
        picker = (
            (segment[:, None] == (column // tail)[None, :])
            & (offset[:, None] < shift)
            & ((column % tail)[None, :] == tail - shift + offset[:, None])
        ).astype(BF)
        lagged.append(local + jnp.dot(picker, tail_rows, preferred_element_type=F32).astype(BF))
    lagged.append(branch_joined)
    b_values, b_b, b_c = split_conv(conv_silu(lagged, weights), channels, heads)
    b_step, b_log, b_cum = decays(branch_dt, decay_rate)
    mask = (segment[:, None] == segment[None, :]) & live[:, None] & (row[None, :] <= row[:, None])
    b_mixed = intra(b_values, b_b, b_c, b_step, b_cum, mask)
    starts = pick(b_cum - b_log, my_start)
    gap = b_cum - jnp.where(inside[0][None, :], starts[0][:, None], starts[1][:, None])
    seed_weight = jnp.where(live[None, :], jnp.exp(jnp.where(live[None, :], gap, 0.0)), 0.0)
    shape = (heads, channels // heads, n_state)
    mixed = mixed + from_state(c_rows, back[:, :rows].reshape(shape), jnp.exp(cumulative))
    for slot in range(BR_PER):
        seed = back[:, (slot + 1) * rows : (slot + 2) * rows].reshape(shape)
        b_mixed = b_mixed + from_state(
            b_c, seed, jnp.where(inside[slot][None, :], seed_weight, 0.0)
        )

    def gate(mixed, values, z):
        mixed = mixed + skip[None, :, None] * values.astype(F32)
        gated = mixed.reshape(length, -1) * jax.nn.silu(z.astype(F32))
        return (gated, jnp.sum(gated * gated, axis=1))

    gated, squares = gate(mixed, values, prefix_z)
    b_gated, b_squares = gate(b_mixed, b_values, branch_z)
    every = lax.all_gather(jnp.stack([squares, b_squares])[None], "tp", axis=0, tiled=True)
    factor = lax.rsqrt(jnp.sum(every, axis=0) / (channels * lax.axis_size("tp")) + EPSILON)
    prefix_out = (gated * factor[0][:, None] * norm_gain[None, :]).astype(BF)
    branch_out = (b_gated * factor[1][:, None] * norm_gain[None, :]).astype(BF)
    return (prefix_out, jnp.where(live[:, None], branch_out, jnp.zeros_like(branch_out)))


def solution(mesh):
    both = P(("ctx", "tp"), None)
    in_specs = (
        P("ctx", "tp"),
        P("ctx", "tp"),
        both,
        P("tp", "ctx"),
        P("ctx", "tp"),
        P("ctx", "tp"),
        both,
        P("tp", "ctx"),
        P(None, "tp"),
        P(),
        P("tp"),
        P("tp"),
        P("tp"),
        P(),
        P(),
        P(),
        P(),
    )
    out_specs = (P("ctx", "tp"), P("ctx", "tp"))
    return jax.shard_map(body, mesh=mesh, in_specs=in_specs, out_specs=out_specs, check_vma=False)
```

profile of v0, /device:TPU:1, one launch (start us, length us, event | category | flops | bytes accessed | tf_op | source)
XLA Modules:
  0.0 158.5 jit_solution(17156961118969503318)
XLA Ops:
  1.4 25.2 %all_gather.6 = bf16[256,512]{1,0:T(8,128)(2,1)S(1)} all-gather(bf16[16,512]{1,0:T(8,128)(2,1)S(1)} %pad_maximum_fusion.3), channel_id=1, replica_groups=mesh['ctx'=32,'tp'=16] {'tp'}, dimensions={0}, use_global_device_ids=true | all-gather | bytes 278528 | tf_op jit(solution)/shard_map/all_gather | solution.py:109
  27.3 3.2 %collective-permute-start = (bf16[3,768]{1,0:T(4,128)(2,1)S(1)}, bf16[3,768]{1,0:T(4,128)(2,1)S(1)}, u32[]{:S(2)}, u32[]{:S(2)}) collective-permute-start(bf16[3,768]{1,0:T(4,128)(2,1)S(1)} %fusion.90), channel_id=1, source_target_pairs={{0,16},{16,32},{32,48},{48,64},{64,80},{80,96},{96,112},{112,128},... | collective-permute-start | bytes 13832 | tf_op jit(solution)/shard_map/ppermute | solution.py:113
  33.1 1.3 compare_select_fusion.1
  34.4 1.5 bitcast_exponential_fusion
  36.7 1.4 select_reduce_fusion.2
  43.1 1.0 maximum_maximum_fusion
  47.7 3.7 %concatenate.39 = bf16[32,199,128]{2,1,0:T(8,128)(2,1)S(1)} concatenate(bf16[32,16,128]{2,1,0:T(8,128)(2,1)} %get-tuple-element.25, bf16[32,16,128]{2,1,0:T(8,128)(2,1)} %get-tuple-element.24, bf16[32,128,128]{2,1,0:T(8,128)(2,1)S(1)} %bitcast.88, bf16[32,36,128]{2,1,0:T(8,128)(2,1)S(1)} %reshape.471, bf16[32,1,128]{2,1,0:T(2,128)(2,1)S(1)} %copy.56, bf16[32,1,128]{2,1,0:T(2,128)(2,1)} %copy.57, ...), dimensions={1} | concatenate | bytes 3260416 | tf_op jit(solution)/shard_map/concatenate | solution.py:165
  51.4 1.3 pad.12
  52.7 8.9 %all-to-all-start = ((bf16[32,208,128]{2,1,0:T(8,128)(2,1)}), bf16[32,208,128]{2,1,0:T(8,128)(2,1)S(1)}, u32[]{:S(2)}, u32[]{:S(2)}) async-start(bf16[32,208,128]{2,1,0:T(8,128)(2,1)} %pad.12), calls=%async_computation | async-start | bytes 3407872 | tf_op jit(solution)/shard_map/all_to_all | solution.py:167
  65.5 0.8 fusion.42
  69.7 0.9 fusion.59
  70.6 31.0 %all-to-all-done = bf16[32,208,128]{2,1,0:T(8,128)(2,1)S(1)} async-done(((bf16[32,208,128]{2,1,0:T(8,128)(2,1)}), bf16[32,208,128]{2,1,0:T(8,128)(2,1)S(1)}, u32[]{:S(2)}, u32[]{:S(2)}) %all-to-all-start) | async-done | bytes 1703968 | tf_op jit(solution)/shard_map/all_to_all | solution.py:167
  103.0 1.1 slice.184
  104.1 1.5 reshape.475
  105.7 1.4 select_reduce_fusion.5
  107.0 1.4 copy.59
  108.4 0.8 subtract_reduce_fusion
  109.2 0.9 select_reduce_fusion
  110.2 1.1 fusion.46
  112.0 0.9 fusion.99
  112.9 0.9 convolution_add_fusion
  114.4 0.9 copy.66
  116.1 7.5 %all-to-all-start.1 = ((bf16[32,48,128]{2,1,0:T(8,128)(2,1)}), bf16[32,48,128]{2,1,0:T(8,128)(2,1)S(1)}, u32[]{:S(2)}, u32[]{:S(2)}) async-start(bf16[32,48,128]{2,1,0:T(8,128)(2,1)} %pad_maximum_fusion.2), calls=%async_computation.1 | async-start | bytes 786432 | tf_op jit(solution)/shard_map/all_to_all | solution.py:205
  123.7 1.5 fusion.16
  125.2 1.1 fusion.19
  127.2 0.8 copy.61
  128.0 0.9 fusion.52
  128.9 5.3 %all-to-all-done.1 = bf16[32,48,128]{2,1,0:T(8,128)(2,1)S(1)} async-done(((bf16[32,48,128]{2,1,0:T(8,128)(2,1)}), bf16[32,48,128]{2,1,0:T(8,128)(2,1)S(1)}, u32[]{:S(2)}, u32[]{:S(2)}) %all-to-all-start.1) | async-done | bytes 393248 | tf_op jit(solution)/shard_map/all_to_all | solution.py:205
  136.4 0.8 fusion.7
  137.9 18.7 %all-gather.1 = f32[16,2,256]{2,1,0:T(2,128)S(1)} all-gather(f32[1,2,256]{2,1,0:T(2,128)S(1)} %maximum_bitcast_fusion), channel_id=2, replica_groups=mesh['ctx'=32,'tp'=16] {'tp'}, dimensions={0}, use_global_device_ids=true | all-gather | bytes 34816 | tf_op jit(solution)/shard_map/all_gather | solution.py:250
  156.7 0.9 fusion.45
  157.6 0.9 multiply_convert_fusion.5
  (200 shorter events, 27.4 us)
Async XLA Ops:
  0.6 43.6 %copy-start.1 = (bf16[256,512]{1,0:T(8,128)(2,1)S(1)}, bf16[256,512]{1,0:T(8,128)(2,1)}, u32[]{:S(2)}) copy-start(bf16[256,512]{1,0:T(8,128)(2,1)} %param.17) | copy-start | bytes 786436
  27.3 15.8 %collective-permute-start = (bf16[3,768]{1,0:T(4,128)(2,1)S(1)}, bf16[3,768]{1,0:T(4,128)(2,1)S(1)}, u32[]{:S(2)}, u32[]{:S(2)}) collective-permute-start(bf16[3,768]{1,0:T(4,128)(2,1)S(1)} %fusion.90), channel_id=1, source_target_pairs={{0,16},{16,32},{32,48},{48,64},{64,80},{80,96},{96,112},{112,128},... | collective-permute-start | bytes 13832 | tf_op jit(solution)/shard_map/ppermute | solution.py:113
  31.2 8.6 %copy-start.30 = (s32[8]{0:T(128)}, s32[8]{0:T(128)S(1)}, u32[]{:S(2)}) copy-start(s32[8]{0:T(128)S(1)} %get-tuple-element.16) | copy-start | bytes 100
  32.1 12.1 %copy-start.34 = (pred[8,32]{1,0:T(8,128)(4,1)}, pred[8,32]{1,0:T(8,128)(4,1)S(1)}, u32[]{:S(2)}) copy-start(pred[8,32]{1,0:T(8,128)(4,1)S(1)} %iota_compare_fusion.14) | copy-start | bytes 772
  32.2 12.0 %copy-start.35 = (pred[8,8]{1,0:T(8,128)(4,1)}, pred[8,8]{1,0:T(8,128)(4,1)S(1)}, u32[]{:S(2)}) copy-start(pred[8,8]{1,0:T(8,128)(4,1)S(1)} %iota_compare_fusion.13) | copy-start | bytes 196
  36.0 8.7 %copy-start.20 = (f32[8,256]{1,0:T(8,128)}, f32[8,256]{1,0:T(8,128)S(1)}, u32[]{:S(2)}) copy-start(f32[8,256]{1,0:T(8,128)S(1)} %get-tuple-element.54) | copy-start | bytes 24580
  52.7 9.0 %copy-start.11 = (pred[8,32,8]{2,1,0:T(8,128)(4,1)S(1)}, pred[8,32,8]{2,1,0:T(8,128)(4,1)}, u32[]{:S(2)}) copy-start(pred[8,32,8]{2,1,0:T(8,128)(4,1)} %broadcast_and_fusion) | copy-start | bytes 6148
  52.7 9.7 %copy-start.42 = (s32[64]{0:T(128)S(1)}, s32[64]{0:T(128)}, u32[]{:S(2)}) copy-start(s32[64]{0:T(128)} %param.33) | copy-start | bytes 772
  52.7 9.7 %copy-start.43 = (s32[64]{0:T(128)S(1)}, s32[64]{0:T(128)}, u32[]{:S(2)}) copy-start(s32[64]{0:T(128)} %get-tuple-element.11) | copy-start | bytes 772
  52.7 9.7 %copy-start.46 = (s32[64]{0:T(128)S(1)}, s32[64]{0:T(128)}, u32[]{:S(2)}) copy-start(s32[64]{0:T(128)} %copy-done.45) | copy-start | bytes 772
  52.7 10.6 %copy-start.49 = (f32[8,256]{1,0:T(8,128)S(1)}, f32[8,256]{1,0:T(8,128)}, u32[]{:S(2)}) copy-start(f32[8,256]{1,0:T(8,128)} %param.24) | copy-start | bytes 24580
  52.7 10.6 %copy-start.52 = (f32[8]{0:T(128)S(1)}, f32[8]{0:T(128)}, u32[]{:S(2)}) copy-start(f32[8]{0:T(128)} %copy-done.51) | copy-start | bytes 100
  52.7 12.0 %copy-start = (bf16[256,512]{1,0:T(8,128)(2,1)S(1)}, bf16[256,512]{1,0:T(8,128)(2,1)}, u32[]{:S(2)}) copy-start(bf16[256,512]{1,0:T(8,128)(2,1)} %param.21) | copy-start | bytes 786436
  52.7 48.9 %all-to-all-start = ((bf16[32,208,128]{2,1,0:T(8,128)(2,1)}), bf16[32,208,128]{2,1,0:T(8,128)(2,1)S(1)}, u32[]{:S(2)}, u32[]{:S(2)}) async-start(bf16[32,208,128]{2,1,0:T(8,128)(2,1)} %pad.12), calls=%async_computation | async-start | bytes 3407872 | tf_op jit(solution)/shard_map/all_to_all | solution.py:167
  62.7 40.3 %copy-start.36 = (pred[256]{0:T(512)(128)(4,1)}, pred[256]{0:T(512)(128)(4,1)S(1)}, u32[]{:S(2)}) copy-start(pred[256]{0:T(512)(128)(4,1)S(1)} %or.10) | copy-start | bytes 772
  64.0 39.1 %copy-start.32 = (f32[8,256]{1,0:T(8,128)}, f32[8,256]{1,0:T(8,128)S(1)}, u32[]{:S(2)}) copy-start(f32[8,256]{1,0:T(8,128)S(1)} %get-tuple-element.52) | copy-start | bytes 24580
  67.1 35.9 %copy-start.22 = (s32[256]{0:T(256)}, s32[256]{0:T(256)S(1)}, u32[]{:S(2)}) copy-start(s32[256]{0:T(256)S(1)} %select_select_fusion.1) | copy-start | bytes 3076
  112.9 10.8 %copy-start.17 = (f32[768]{0:T(1024)S(1)}, f32[768]{0:T(1024)}, u32[]{:S(2)}) copy-start(f32[768]{0:T(1024)} %copy-done.16) | copy-start | bytes 9220
  112.9 10.8 %copy-start.23 = (s32[256]{0:T(256)S(1)}, s32[256]{0:T(256)}, u32[]{:S(2)}) copy-start(s32[256]{0:T(256)} %copy-done.22) | copy-start | bytes 3076
  113.8 11.4 %copy-start.2 = (bf16[255,768]{1,0:T(8,128)(2,1)S(1)}, bf16[255,768]{1,0:T(8,128)(2,1)}, u32[]{:S(2)}) copy-start(bf16[255,768]{1,0:T(8,128)(2,1)} %fusion.42) | copy-start | bytes 1175044
  113.8 11.4 %copy-start.15 = (f32[768]{0:T(1024)S(1)}, f32[768]{0:T(1024)}, u32[]{:S(2)}) copy-start(f32[768]{0:T(1024)} %copy-done.14) | copy-start | bytes 9220
  115.3 11.0 %copy-start.25 = (f32[768]{0:T(1024)S(1)}, f32[768]{0:T(1024)}, u32[]{:S(2)}) copy-start(f32[768]{0:T(1024)} %copy-done.24) | copy-start | bytes 9220
  116.1 10.2 %copy-start.27 = (f32[768]{0:T(1024)S(1)}, f32[768]{0:T(1024)}, u32[]{:S(2)}) copy-start(f32[768]{0:T(1024)} %copy-done.26) | copy-start | bytes 9220
  116.1 10.2 %copy-start.38 = (s32[6]{0:T(128)S(1)}, s32[6]{0:T(128)}, u32[]{:S(2)}) copy-start(s32[6]{0:T(128)} %get-tuple-element.55) | copy-start | bytes 76
  116.1 10.2 %copy-start.39 = (s32[6]{0:T(128)S(1)}, s32[6]{0:T(128)}, u32[]{:S(2)}) copy-start(s32[6]{0:T(128)} %get-tuple-element.56) | copy-start | bytes 76
  116.1 10.2 %copy-start.44 = (s32[256]{0:T(256)S(1)}, s32[256]{0:T(256)}, u32[]{:S(2)}) copy-start(s32[256]{0:T(256)} %get-tuple-element.43) | copy-start | bytes 3076
  116.1 10.2 %copy-start.47 = (pred[256]{0:T(512)(128)(4,1)S(1)}, pred[256]{0:T(512)(128)(4,1)}, u32[]{:S(2)}) copy-start(pred[256]{0:T(512)(128)(4,1)} %get-tuple-element.37) | copy-start | bytes 772
  116.1 10.2 %copy-start.48 = (pred[256]{0:T(512)(128)(4,1)S(1)}, pred[256]{0:T(512)(128)(4,1)}, u32[]{:S(2)}) copy-start(pred[256]{0:T(512)(128)(4,1)} %get-tuple-element.38) | copy-start | bytes 772
  116.1 18.0 %all-to-all-start.1 = ((bf16[32,48,128]{2,1,0:T(8,128)(2,1)}), bf16[32,48,128]{2,1,0:T(8,128)(2,1)S(1)}, u32[]{:S(2)}, u32[]{:S(2)}) async-start(bf16[32,48,128]{2,1,0:T(8,128)(2,1)} %pad_maximum_fusion.2), calls=%async_computation.1 | async-start | bytes 786432 | tf_op jit(solution)/shard_map/all_to_all | solution.py:205
  127.1 7.4 %copy-start.6 = (bf16[256,512]{0,1:T(8,128)(2,1)S(1)}, bf16[256,512]{0,1:T(8,128)(2,1)}, u32[]{:S(2)}) copy-start(bf16[256,512]{0,1:T(8,128)(2,1)} %copy-done.5) | copy-start | bytes 786436
  137.2 19.5 %copy-start.29 = (f32[512]{0:T(512)S(1)}, f32[512]{0:T(512)}, u32[]{:S(2)}) copy-start(f32[512]{0:T(512)} %param.29) | copy-start | bytes 6148
  137.2 19.5 %copy-start.37 = (pred[256]{0:T(512)(128)(4,1)S(1)}, pred[256]{0:T(512)(128)(4,1)}, u32[]{:S(2)}) copy-start(pred[256]{0:T(512)(128)(4,1)} %copy-done.36) | copy-start | bytes 772
  (25 other events, 78.7 us)
where the time goes:
time: 160 us; the launch traced here: 158 us
  blocking collectives  43.9 us (27%)
  waiting for transfers between devices  36.3 us (23%)
  other arithmetic  25.4 us (16%)
  starting transfers between devices  19.6 us (12%)
  local copies, waits for them, and re-layouts  17.9 us (11%)
  matrix products  13.9 us (9%)
    all_to_all x1, waiting for transfers between devices, body(): got = lax.all_to_all(sent, 'ctx', 0, 0, tiled=True)  31 us
    all_gather x1, blocking collectives, body(): lax.all_gather(jnp.concatenate([prefix_bc, branch_bc], axis=1), 'tp', axi...  25.2 us
    all_gather x1, blocking collectives, body(): lax.all_gather(jnp.stack([squares, b_squares])[None], 'tp', axis=0, tiled...  18.7 us
    all_to_all x1, starting transfers between devices, body(): got = lax.all_to_all(sent, 'ctx', 0, 0, tiled=True)  8.92 us
    all_to_all x1, starting transfers between devices, body(): back = lax.all_to_all(back, 'ctx', 0, 0, tiled=True)  7.45 us
    all_to_all x1, waiting for transfers between devices, body(): back = lax.all_to_all(back, 'ctx', 0, 0, tiled=True)  5.25 us
    concatenate x1, local copies, waits for them, and re-layouts, body(): sent = jnp.concatenate(pieces, axis=1)  3.65 us
    dot_general x3, matrix products, body(): jnp.dot(picker, tail_rows, preferred_element_type=F32).astype(BF)  3.24 us
  transfers between devices with their start and end apart: 3, of which 2 were waited for; matrix products, arithmetic and copies ran while one was open for 17% of the time, Pallas kernels for 0%

commit v1 on v0

--- a/solution.py
+++ b/solution.py
@@ -106,9 +106,22 @@
     taps = weights.shape[0]
     tail = taps - 1
     row_width = channels + width
-    gathered = lax.all_gather(
-        jnp.concatenate([prefix_bc, branch_bc], axis=1), "tp", axis=0, tiled=True
-    )
+    array_2 = jnp.concatenate([prefix_bc, branch_bc], axis=1)
+    ways, here, turn = (lax.axis_size("tp"), lax.axis_index("tp"), array_2.shape[0])
+    shape_2 = [n * ways if d == 0 else n for d, n in enumerate(array_2.shape)]
+    full = lax.dynamic_update_slice_in_dim(
+        jnp.zeros(shape_2, array_2.dtype), array_2, here * turn, axis=0
+    )
+    going_up = going_down = array_2
+    for far in range(1, ways // 2 + 1):
+        going_up = lax.ppermute(going_up, "tp", [(d, (d + 1) % ways) for d in range(ways)])
+        full = lax.dynamic_update_slice_in_dim(full, going_up, (here - far) % ways * turn, axis=0)
+        if 2 * far < ways:
+            going_down = lax.ppermute(going_down, "tp", [(d, (d - 1) % ways) for d in range(ways)])
+            full = lax.dynamic_update_slice_in_dim(
+                full, going_down, (here + far) % ways * turn, axis=0
+            )
+    gathered = full
     joined = jnp.concatenate([prefix_x, gathered[:, :width]], axis=1)
     before = lax.ppermute(joined[length - tail :], "ctx", [(i, i + 1) for i in range(n_ctx - 1)])
     extended = jnp.concatenate([before, joined], axis=0)

time: 160 us -> 170 us (1.062)
  starting transfers between devices: 19.6 us -> 50.4 us
  blocking collectives: 43.9 us -> 25.6 us
  other arithmetic: 25.4 us -> 20.3 us
  waiting for transfers between devices: 36.3 us -> 39.9 us
  local copies, waits for them, and re-layouts: 17.9 us -> 16 us
    ppermute x0 -> x15, starting transfers between devices: none -> 27.7 us  [the longest x7 24.2 us: body(): lax.ppermute(going_down, 'tp', [(d, (d - 1) % ways) for d in range(ways)])]
    all_gather x1 -> x0, blocking collectives: 25.2 us -> none  [body(): lax.all_gather(jnp.concatenate([prefix_bc, branch_bc], axis=1), 'tp', axi...]
    ppermute x0 -> x15, waiting for transfers between devices: none -> 9.16 us  [the longest x8 8.03 us: body(): lax.ppermute(going_up, 'tp', [(d, (d + 1) % ways) for d in range(ways)])]
    all_gather x1, blocking collectives: 18.7 us -> 25.6 us  [body(): lax.all_gather(jnp.stack([squares, b_squares])[None], 'tp', axis=0, tiled...]
    all_to_all x1, waiting for transfers between devices: 31 us -> 25.2 us  [body(): got = lax.all_to_all(sent, 'ctx', 0, 0, tiled=True)]
    all_to_all x1, starting transfers between devices: 8.92 us -> 10.7 us  [body(): got = lax.all_to_all(sent, 'ctx', 0, 0, tiled=True)]
  transfers between devices with their start and end apart: 3 -> 18, of which waited for: 2 -> 15; matrix products, arithmetic and copies ran while one was open for 17% -> 15% of each run, Pallas kernels for 0% -> 0%
where the time goes in v1:
time: 170 us; the launch traced here: 169 us
  starting transfers between devices  50.4 us (30%)
  waiting for transfers between devices  39.9 us (23%)
  blocking collectives  25.6 us (15%)
  other arithmetic  20.3 us (12%)
  local copies, waits for them, and re-layouts  16 us (9%)
  matrix products  15.2 us (9%)
    all_gather x1, blocking collectives, body(): lax.all_gather(jnp.stack([squares, b_squares])[None], 'tp', axis=0, tiled...  25.6 us
    all_to_all x1, waiting for transfers between devices, body(): got = lax.all_to_all(sent, 'ctx', 0, 0, tiled=True)  25.2 us
    ppermute x7, starting transfers between devices, body(): lax.ppermute(going_down, 'tp', [(d, (d - 1) % ways) for d in range(ways)])  24.2 us
    all_to_all x1, starting transfers between devices, body(): got = lax.all_to_all(sent, 'ctx', 0, 0, tiled=True)  10.7 us
    all_to_all x1, starting transfers between devices, body(): back = lax.all_to_all(back, 'ctx', 0, 0, tiled=True)  8.77 us
    ppermute x8, waiting for transfers between devices, body(): lax.ppermute(going_up, 'tp', [(d, (d + 1) % ways) for d in range(ways)])  8.03 us
    all_to_all x1, waiting for transfers between devices, body(): back = lax.all_to_all(back, 'ctx', 0, 0, tiled=True)  5.55 us
    dot_general x3, matrix products, body(): jnp.dot(picker, tail_rows, preferred_element_type=F32).astype(BF)  4.02 us
  transfers between devices with their start and end apart: 18, of which 15 were waited for; matrix products, arithmetic and copies ran while one was open for 15% of the time, Pallas kernels for 0%

profile of v1, /device:TPU:1, one launch (start us, length us, event | category | flops | bytes accessed | tf_op | source)
XLA Modules:
  0.0 168.9 jit_solution(15988136309436710084)
XLA Ops:
  2.1 3.5 %collective-permute-start = (bf16[16,512]{1,0:T(8,128)(2,1)S(1)}, bf16[16,512]{1,0:T(8,128)(2,1)S(1)}, u32[]{:S(2)}, u32[]{:S(2)}) collective-permute-start(bf16[16,512]{1,0:T(8,128)(2,1)S(1)} %constant_dynamic-update-slice_fusion.2), channel_id=1, source_target_pairs={{0,1},{1,2},{2,3},{3,4},{4,5},{5,6},{6,7},{7,8},{8,9},{9,10},{10,1... | collective-permute-start | bytes 49160 | tf_op jit(solution)/shard_map/ppermute | solution.py:117
  5.6 3.4 %collective-permute-start.1 = (bf16[16,512]{1,0:T(8,128)(2,1)S(1)}, bf16[16,512]{1,0:T(8,128)(2,1)S(1)}, u32[]{:S(2)}, u32[]{:S(2)}) collective-permute-start(bf16[16,512]{1,0:T(8,128)(2,1)S(1)} %constant_dynamic-update-slice_fusion.2), channel_id=1, source_target_pairs={{0,15},{1,0},{2,1},{3,2},{4,3},{5,4},{6,5},{7,6},{8,7},{9,8},{10,9... | collective-permute-start | bytes 49160 | tf_op jit(solution)/shard_map/ppermute | solution.py:120
  11.2 1.3 compare_select_fusion.1
  13.2 1.5 bitcast_exponential_fusion
  15.1 1.4 select_reduce_fusion.2
  20.2 3.1 %collective-permute-start.3 = (bf16[16,512]{1,0:T(8,128)(2,1)S(1)}, bf16[16,512]{1,0:T(8,128)(2,1)S(1)}, u32[]{:S(2)}, u32[]{:S(2)}) collective-permute-start(bf16[16,512]{1,0:T(8,128)(2,1)S(1)} %collective-permute-done.1), channel_id=1, source_target_pairs={{0,15},{1,0},{2,1},{3,2},{4,3},{5,4},{6,5},{7,6},{8,7},{9,8},{10,9... | collective-permute-start | bytes 49160 | tf_op jit(solution)/shard_map/ppermute | solution.py:120
  24.1 3.5 %collective-permute-start.5 = (bf16[16,512]{1,0:T(8,128)(2,1)S(1)}, bf16[16,512]{1,0:T(8,128)(2,1)S(1)}, u32[]{:S(2)}, u32[]{:S(2)}) collective-permute-start(bf16[16,512]{1,0:T(8,128)(2,1)S(1)} %collective-permute-done.3), channel_id=1, source_target_pairs={{0,15},{1,0},{2,1},{3,2},{4,3},{5,4},{6,5},{7,6},{8,7},{9,8},{10,9... | collective-permute-start | bytes 49160 | tf_op jit(solution)/shard_map/ppermute | solution.py:120
  28.5 3.5 %collective-permute-start.7 = (bf16[16,512]{1,0:T(8,128)(2,1)S(1)}, bf16[16,512]{1,0:T(8,128)(2,1)S(1)}, u32[]{:S(2)}, u32[]{:S(2)}) collective-permute-start(bf16[16,512]{1,0:T(8,128)(2,1)S(1)} %collective-permute-done.5), channel_id=1, source_target_pairs={{0,15},{1,0},{2,1},{3,2},{4,3},{5,4},{6,5},{7,6},{8,7},{9,8},{10,9... | collective-permute-start | bytes 49160 | tf_op jit(solution)/shard_map/ppermute | solution.py:120
  32.9 3.5 %collective-permute-start.9 = (bf16[16,512]{1,0:T(8,128)(2,1)S(1)}, bf16[16,512]{1,0:T(8,128)(2,1)S(1)}, u32[]{:S(2)}, u32[]{:S(2)}) collective-permute-start(bf16[16,512]{1,0:T(8,128)(2,1)S(1)} %collective-permute-done.7), channel_id=1, source_target_pairs={{0,15},{1,0},{2,1},{3,2},{4,3},{5,4},{6,5},{7,6},{8,7},{9,8},{10,9... | collective-permute-start | bytes 49160 | tf_op jit(solution)/shard_map/ppermute | solution.py:120
  37.3 3.5 %collective-permute-start.11 = (bf16[16,512]{1,0:T(8,128)(2,1)S(1)}, bf16[16,512]{1,0:T(8,128)(2,1)S(1)}, u32[]{:S(2)}, u32[]{:S(2)}) collective-permute-start(bf16[16,512]{1,0:T(8,128)(2,1)S(1)} %collective-permute-done.9), channel_id=1, source_target_pairs={{0,15},{1,0},{2,1},{3,2},{4,3},{5,4},{6,5},{7,6},{8,7},{9,8},{10,9... | collective-permute-start | bytes 49160 | tf_op jit(solution)/shard_map/ppermute | solution.py:120
  41.6 3.5 %collective-permute-start.13 = (bf16[16,512]{1,0:T(8,128)(2,1)S(1)}, bf16[16,512]{1,0:T(8,128)(2,1)S(1)}, u32[]{:S(2)}, u32[]{:S(2)}) collective-permute-start(bf16[16,512]{1,0:T(8,128)(2,1)S(1)} %collective-permute-done.11), channel_id=1, source_target_pairs={{0,15},{1,0},{2,1},{3,2},{4,3},{5,4},{6,5},{7,6},{8,7},{9,8},{10,9... | collective-permute-start | bytes 49160 | tf_op jit(solution)/shard_map/ppermute | solution.py:120
  46.0 4.2 %collective-permute-done.14 = bf16[16,512]{1,0:T(8,128)(2,1)S(1)} collective-permute-done((bf16[16,512]{1,0:T(8,128)(2,1)S(1)}, bf16[16,512]{1,0:T(8,128)(2,1)S(1)}, u32[]{:S(2)}, u32[]{:S(2)}) %collective-permute-start.14) | collective-permute-done | bytes 16416 | tf_op jit(solution)/shard_map/ppermute | solution.py:117
  50.2 3.2 %collective-permute-start.15 = (bf16[3,768]{1,0:T(4,128)(2,1)S(1)}, bf16[3,768]{1,0:T(4,128)(2,1)S(1)}, u32[]{:S(2)}, u32[]{:S(2)}) collective-permute-start(bf16[3,768]{1,0:T(4,128)(2,1)S(1)} %fusion.90), channel_id=1, source_target_pairs={{0,16},{16,32},{32,48},{48,64},{64,80},{80,96},{96,112},{112,128},... | collective-permute-start | bytes 13832 | tf_op jit(solution)/shard_map/ppermute | solution.py:126
  58.6 3.7 %concatenate.39 = bf16[32,199,128]{2,1,0:T(8,128)(2,1)S(1)} concatenate(bf16[32,16,128]{2,1,0:T(8,128)(2,1)} %get-tuple-element.25, bf16[32,16,128]{2,1,0:T(8,128)(2,1)} %get-tuple-element.24, bf16[32,128,128]{2,1,0:T(8,128)(2,1)S(1)} %bitcast.88, bf16[32,36,128]{2,1,0:T(8,128)(2,1)S(1)} %reshape.471, bf16[32,1,128]{2,1,0:T(2,128)(2,1)S(1)} %copy.56, bf16[32,1,128]{2,1,0:T(2,128)(2,1)} %copy.57, ...), dimensions={1} | concatenate | bytes 3260416 | tf_op jit(solution)/shard_map/concatenate | solution.py:178
  62.2 1.3 pad.12
  63.6 10.7 %all-to-all-start = ((bf16[32,208,128]{2,1,0:T(8,128)(2,1)}), bf16[32,208,128]{2,1,0:T(8,128)(2,1)S(1)}, u32[]{:S(2)}, u32[]{:S(2)}) async-start(bf16[32,208,128]{2,1,0:T(8,128)(2,1)} %pad.12), calls=%async_computation | async-start | bytes 3407872 | tf_op jit(solution)/shard_map/all_to_all | solution.py:180
  83.3 25.2 %all-to-all-done = bf16[32,208,128]{2,1,0:T(8,128)(2,1)S(1)} async-done(((bf16[32,208,128]{2,1,0:T(8,128)(2,1)}), bf16[32,208,128]{2,1,0:T(8,128)(2,1)S(1)}, u32[]{:S(2)}, u32[]{:S(2)}) %all-to-all-start) | async-done | bytes 1703968 | tf_op jit(solution)/shard_map/all_to_all | solution.py:180
  110.5 0.9 fusion.99
  111.4 1.1 slice.184
  112.5 1.5 reshape.475
  114.0 1.1 convolution_add_fusion
  115.1 1.1 convolution_convert_fusion
  116.4 0.9 copy.66
  118.1 8.8 %all-to-all-start.1 = ((bf16[32,48,128]{2,1,0:T(8,128)(2,1)}), bf16[32,48,128]{2,1,0:T(8,128)(2,1)S(1)}, u32[]{:S(2)}, u32[]{:S(2)}) async-start(bf16[32,48,128]{2,1,0:T(8,128)(2,1)} %pad_maximum_fusion.2), calls=%async_computation.1 | async-start | bytes 786432 | tf_op jit(solution)/shard_map/all_to_all | solution.py:218
  127.0 1.5 fusion.19
  128.5 1.1 fusion.16
  129.6 1.4 multiply_convert_fusion.2
  131.4 5.6 %all-to-all-done.1 = bf16[32,48,128]{2,1,0:T(8,128)(2,1)S(1)} async-done(((bf16[32,48,128]{2,1,0:T(8,128)(2,1)}), bf16[32,48,128]{2,1,0:T(8,128)(2,1)S(1)}, u32[]{:S(2)}, u32[]{:S(2)}) %all-to-all-start.1) | async-done | bytes 393248 | tf_op jit(solution)/shard_map/all_to_all | solution.py:218
  138.9 1.8 %fusion.6 = f32[256,8,64]{0,2,1:T(8,128)S(1)} fusion(f32[256,8,64]{0,2,1:T(8,128)S(1)} %convolution_multiply_fusion.2, bf16[256,8,64]{0,2,1:T(8,128)(2,1)S(1)} %bitcast.91, f32[8,256]{1,0:T(8,128)S(1)} %copy-done.26, f32[8,256]{1,0:T(8,128)S(1)} %copy-done.17, f32[256,256]{1,0:T(8,128)} %fusion.59, pred[256,256]{1,0:T(8,128)(4,1)S(1)} %copy-done.9, ...), kind=kOutput, calls=%fused_computation.20 | convolution fusion | flops 70778880 | bytes 1654816 | tf_op jit(solution)/shard_map/hts,shp->thp/dot_general | solution.py:41
  141.4 25.6 %all-gather.1 = f32[16,2,256]{2,1,0:T(2,128)S(1)} all-gather(f32[1,2,256]{2,1,0:T(2,128)S(1)} %maximum_bitcast_fusion), channel_id=2, replica_groups=mesh['ctx'=32,'tp'=16] {'tp'}, dimensions={0}, use_global_device_ids=true | all-gather | bytes 34816 | tf_op jit(solution)/shard_map/all_gather | solution.py:263
  167.0 0.9 multiply_convert_fusion.5
  167.9 0.9 fusion.45
  (229 shorter events, 33.0 us)
Async XLA Ops:
  0.6 49.6 %copy-start.1 = (bf16[256,512]{1,0:T(8,128)(2,1)S(1)}, bf16[256,512]{1,0:T(8,128)(2,1)}, u32[]{:S(2)}) copy-start(bf16[256,512]{1,0:T(8,128)(2,1)} %param.17) | copy-start | bytes 786436
  2.1 18.1 %collective-permute-start = (bf16[16,512]{1,0:T(8,128)(2,1)S(1)}, bf16[16,512]{1,0:T(8,128)(2,1)S(1)}, u32[]{:S(2)}, u32[]{:S(2)}) collective-permute-start(bf16[16,512]{1,0:T(8,128)(2,1)S(1)} %constant_dynamic-update-slice_fusion.2), channel_id=1, source_target_pairs={{0,1},{1,2},{2,3},{3,4},{4,5},{5,6},{6,7},{7,8},{8,9},{9,10},{10,1... | collective-permute-start | bytes 49160 | tf_op jit(solution)/shard_map/ppermute | solution.py:117
  5.6 14.6 %collective-permute-start.1 = (bf16[16,512]{1,0:T(8,128)(2,1)S(1)}, bf16[16,512]{1,0:T(8,128)(2,1)S(1)}, u32[]{:S(2)}, u32[]{:S(2)}) collective-permute-start(bf16[16,512]{1,0:T(8,128)(2,1)S(1)} %constant_dynamic-update-slice_fusion.2), channel_id=1, source_target_pairs={{0,15},{1,0},{2,1},{3,2},{4,3},{5,4},{6,5},{7,6},{8,7},{9,8},{10,9... | collective-permute-start | bytes 49160 | tf_op jit(solution)/shard_map/ppermute | solution.py:120
  10.5 45.0 %copy-start.29 = (pred[8,32]{1,0:T(8,128)(4,1)}, pred[8,32]{1,0:T(8,128)(4,1)S(1)}, u32[]{:S(2)}) copy-start(pred[8,32]{1,0:T(8,128)(4,1)S(1)} %iota_compare_fusion.14) | copy-start | bytes 772
  14.7 40.8 %copy-start.16 = (f32[8,256]{1,0:T(8,128)}, f32[8,256]{1,0:T(8,128)S(1)}, u32[]{:S(2)}) copy-start(f32[8,256]{1,0:T(8,128)S(1)} %get-tuple-element.54) | copy-start | bytes 24580
  14.8 40.7 %copy-start.31 = (pred[8,8]{1,0:T(8,128)(4,1)}, pred[8,8]{1,0:T(8,128)(4,1)S(1)}, u32[]{:S(2)}) copy-start(pred[8,8]{1,0:T(8,128)(4,1)S(1)} %iota_compare_fusion.13) | copy-start | bytes 196
  20.2 3.8 %collective-permute-start.2 = (bf16[16,512]{1,0:T(8,128)(2,1)S(1)}, bf16[16,512]{1,0:T(8,128)(2,1)S(1)}, u32[]{:S(2)}, u32[]{:S(2)}) collective-permute-start(bf16[16,512]{1,0:T(8,128)(2,1)S(1)} %collective-permute-done), channel_id=1, source_target_pairs={{0,1},{1,2},{2,3},{3,4},{4,5},{5,6},{6,7},{7,8},{8,9},{9,10},{10,1... | collective-permute-start | bytes 49160 | tf_op jit(solution)/shard_map/ppermute | solution.py:117
  20.2 4.0 %collective-permute-start.3 = (bf16[16,512]{1,0:T(8,128)(2,1)S(1)}, bf16[16,512]{1,0:T(8,128)(2,1)S(1)}, u32[]{:S(2)}, u32[]{:S(2)}) collective-permute-start(bf16[16,512]{1,0:T(8,128)(2,1)S(1)} %collective-permute-done.1), channel_id=1, source_target_pairs={{0,15},{1,0},{2,1},{3,2},{4,3},{5,4},{6,5},{7,6},{8,7},{9,8},{10,9... | collective-permute-start | bytes 49160 | tf_op jit(solution)/shard_map/ppermute | solution.py:120
  23.9 4.4 %collective-permute-start.4 = (bf16[16,512]{1,0:T(8,128)(2,1)S(1)}, bf16[16,512]{1,0:T(8,128)(2,1)S(1)}, u32[]{:S(2)}, u32[]{:S(2)}) collective-permute-start(bf16[16,512]{1,0:T(8,128)(2,1)S(1)} %collective-permute-done.2), channel_id=1, source_target_pairs={{0,1},{1,2},{2,3},{3,4},{4,5},{5,6},{6,7},{7,8},{8,9},{9,10},{10,1... | collective-permute-start | bytes 49160 | tf_op jit(solution)/shard_map/ppermute | solution.py:117
  24.1 4.4 %collective-permute-start.5 = (bf16[16,512]{1,0:T(8,128)(2,1)S(1)}, bf16[16,512]{1,0:T(8,128)(2,1)S(1)}, u32[]{:S(2)}, u32[]{:S(2)}) collective-permute-start(bf16[16,512]{1,0:T(8,128)(2,1)S(1)} %collective-permute-done.3), channel_id=1, source_target_pairs={{0,15},{1,0},{2,1},{3,2},{4,3},{5,4},{6,5},{7,6},{8,7},{9,8},{10,9... | collective-permute-start | bytes 49160 | tf_op jit(solution)/shard_map/ppermute | solution.py:120
  28.3 4.4 %collective-permute-start.6 = (bf16[16,512]{1,0:T(8,128)(2,1)S(1)}, bf16[16,512]{1,0:T(8,128)(2,1)S(1)}, u32[]{:S(2)}, u32[]{:S(2)}) collective-permute-start(bf16[16,512]{1,0:T(8,128)(2,1)S(1)} %collective-permute-done.4), channel_id=1, source_target_pairs={{0,1},{1,2},{2,3},{3,4},{4,5},{5,6},{6,7},{7,8},{8,9},{9,10},{10,1... | collective-permute-start | bytes 49160 | tf_op jit(solution)/shard_map/ppermute | solution.py:117
  28.5 4.4 %collective-permute-start.7 = (bf16[16,512]{1,0:T(8,128)(2,1)S(1)}, bf16[16,512]{1,0:T(8,128)(2,1)S(1)}, u32[]{:S(2)}, u32[]{:S(2)}) collective-permute-start(bf16[16,512]{1,0:T(8,128)(2,1)S(1)} %collective-permute-done.5), channel_id=1, source_target_pairs={{0,15},{1,0},{2,1},{3,2},{4,3},{5,4},{6,5},{7,6},{8,7},{9,8},{10,9... | collective-permute-start | bytes 49160 | tf_op jit(solution)/shard_map/ppermute | solution.py:120
  32.7 4.4 %collective-permute-start.8 = (bf16[16,512]{1,0:T(8,128)(2,1)S(1)}, bf16[16,512]{1,0:T(8,128)(2,1)S(1)}, u32[]{:S(2)}, u32[]{:S(2)}) collective-permute-start(bf16[16,512]{1,0:T(8,128)(2,1)S(1)} %collective-permute-done.6), channel_id=1, source_target_pairs={{0,1},{1,2},{2,3},{3,4},{4,5},{5,6},{6,7},{7,8},{8,9},{9,10},{10,1... | collective-permute-start | bytes 49160 | tf_op jit(solution)/shard_map/ppermute | solution.py:117
  32.9 4.4 %collective-permute-start.9 = (bf16[16,512]{1,0:T(8,128)(2,1)S(1)}, bf16[16,512]{1,0:T(8,128)(2,1)S(1)}, u32[]{:S(2)}, u32[]{:S(2)}) collective-permute-start(bf16[16,512]{1,0:T(8,128)(2,1)S(1)} %collective-permute-done.7), channel_id=1, source_target_pairs={{0,15},{1,0},{2,1},{3,2},{4,3},{5,4},{6,5},{7,6},{8,7},{9,8},{10,9... | collective-permute-start | bytes 49160 | tf_op jit(solution)/shard_map/ppermute | solution.py:120
  37.1 4.4 %collective-permute-start.10 = (bf16[16,512]{1,0:T(8,128)(2,1)S(1)}, bf16[16,512]{1,0:T(8,128)(2,1)S(1)}, u32[]{:S(2)}, u32[]{:S(2)}) collective-permute-start(bf16[16,512]{1,0:T(8,128)(2,1)S(1)} %collective-permute-done.8), channel_id=1, source_target_pairs={{0,1},{1,2},{2,3},{3,4},{4,5},{5,6},{6,7},{7,8},{8,9},{9,10},{10,1... | collective-permute-start | bytes 49160 | tf_op jit(solution)/shard_map/ppermute | solution.py:117
  37.3 4.4 %collective-permute-start.11 = (bf16[16,512]{1,0:T(8,128)(2,1)S(1)}, bf16[16,512]{1,0:T(8,128)(2,1)S(1)}, u32[]{:S(2)}, u32[]{:S(2)}) collective-permute-start(bf16[16,512]{1,0:T(8,128)(2,1)S(1)} %collective-permute-done.9), channel_id=1, source_target_pairs={{0,15},{1,0},{2,1},{3,2},{4,3},{5,4},{6,5},{7,6},{8,7},{9,8},{10,9... | collective-permute-start | bytes 49160 | tf_op jit(solution)/shard_map/ppermute | solution.py:120
  41.4 4.4 %collective-permute-start.12 = (bf16[16,512]{1,0:T(8,128)(2,1)S(1)}, bf16[16,512]{1,0:T(8,128)(2,1)S(1)}, u32[]{:S(2)}, u32[]{:S(2)}) collective-permute-start(bf16[16,512]{1,0:T(8,128)(2,1)S(1)} %collective-permute-done.10), channel_id=1, source_target_pairs={{0,1},{1,2},{2,3},{3,4},{4,5},{5,6},{6,7},{7,8},{8,9},{9,10},{10,1... | collective-permute-start | bytes 49160 | tf_op jit(solution)/shard_map/ppermute | solution.py:117
  41.6 4.4 %collective-permute-start.13 = (bf16[16,512]{1,0:T(8,128)(2,1)S(1)}, bf16[16,512]{1,0:T(8,128)(2,1)S(1)}, u32[]{:S(2)}, u32[]{:S(2)}) collective-permute-start(bf16[16,512]{1,0:T(8,128)(2,1)S(1)} %collective-permute-done.11), channel_id=1, source_target_pairs={{0,15},{1,0},{2,1},{3,2},{4,3},{5,4},{6,5},{7,6},{8,7},{9,8},{10,9... | collective-permute-start | bytes 49160 | tf_op jit(solution)/shard_map/ppermute | solution.py:120
  45.8 4.4 %collective-permute-start.14 = (bf16[16,512]{1,0:T(8,128)(2,1)S(1)}, bf16[16,512]{1,0:T(8,128)(2,1)S(1)}, u32[]{:S(2)}, u32[]{:S(2)}) collective-permute-start(bf16[16,512]{1,0:T(8,128)(2,1)S(1)} %collective-permute-done.12), channel_id=1, source_target_pairs={{0,1},{1,2},{2,3},{3,4},{4,5},{5,6},{6,7},{7,8},{8,9},{9,10},{10,1... | collective-permute-start | bytes 49160 | tf_op jit(solution)/shard_map/ppermute | solution.py:117
  50.2 4.7 %collective-permute-start.15 = (bf16[3,768]{1,0:T(4,128)(2,1)S(1)}, bf16[3,768]{1,0:T(4,128)(2,1)S(1)}, u32[]{:S(2)}, u32[]{:S(2)}) collective-permute-start(bf16[3,768]{1,0:T(4,128)(2,1)S(1)} %fusion.90), channel_id=1, source_target_pairs={{0,16},{16,32},{32,48},{48,64},{64,80},{80,96},{96,112},{112,128},... | collective-permute-start | bytes 13832 | tf_op jit(solution)/shard_map/ppermute | solution.py:126
  63.6 16.6 %copy-start = (bf16[256,512]{1,0:T(8,128)(2,1)S(1)}, bf16[256,512]{1,0:T(8,128)(2,1)}, u32[]{:S(2)}) copy-start(bf16[256,512]{1,0:T(8,128)(2,1)} %param.21) | copy-start | bytes 786436
  63.6 44.9 %all-to-all-start = ((bf16[32,208,128]{2,1,0:T(8,128)(2,1)}), bf16[32,208,128]{2,1,0:T(8,128)(2,1)S(1)}, u32[]{:S(2)}, u32[]{:S(2)}) async-start(bf16[32,208,128]{2,1,0:T(8,128)(2,1)} %pad.12), calls=%async_computation | async-start | bytes 3407872 | tf_op jit(solution)/shard_map/all_to_all | solution.py:180
  74.3 34.8 %copy-start.30 = (pred[8,32]{1,0:T(8,128)(4,1)S(1)}, pred[8,32]{1,0:T(8,128)(4,1)}, u32[]{:S(2)}) copy-start(pred[8,32]{1,0:T(8,128)(4,1)} %copy-done.29) | copy-start | bytes 772
  74.3 34.8 %copy-start.32 = (pred[8,8]{1,0:T(8,128)(4,1)S(1)}, pred[8,8]{1,0:T(8,128)(4,1)}, u32[]{:S(2)}) copy-start(pred[8,8]{1,0:T(8,128)(4,1)} %copy-done.31) | copy-start | bytes 196
  75.4 33.5 %copy-start.33 = (pred[256]{0:T(512)(128)(4,1)}, pred[256]{0:T(512)(128)(4,1)S(1)}, u32[]{:S(2)}) copy-start(pred[256]{0:T(512)(128)(4,1)S(1)} %or.10) | copy-start | bytes 772
  77.5 33.0 %copy-start.18 = (s32[256]{0:T(256)}, s32[256]{0:T(256)S(1)}, u32[]{:S(2)}) copy-start(s32[256]{0:T(256)S(1)} %select_select_fusion.1) | copy-start | bytes 3076
  80.1 30.3 %copy-start.25 = (s32[8]{0:T(128)S(1)}, s32[8]{0:T(128)}, u32[]{:S(2)}) copy-start(s32[8]{0:T(128)} %copy-done.24) | copy-start | bytes 100
  115.1 13.3 %copy-start.2 = (bf16[254,768]{1,0:T(8,128)(2,1)S(1)}, bf16[254,768]{1,0:T(8,128)(2,1)}, u32[]{:S(2)}) copy-start(bf16[254,768]{1,0:T(8,128)(2,1)} %fusion.41) | copy-start | bytes 1170436
  115.1 13.3 %copy-start.12 = (f32[768]{0:T(1024)S(1)}, f32[768]{0:T(1024)}, u32[]{:S(2)}) copy-start(f32[768]{0:T(1024)} %copy-done.11) | copy-start | bytes 9220
  118.1 18.9 %all-to-all-start.1 = ((bf16[32,48,128]{2,1,0:T(8,128)(2,1)}), bf16[32,48,128]{2,1,0:T(8,128)(2,1)S(1)}, u32[]{:S(2)}, u32[]{:S(2)}) async-start(bf16[32,48,128]{2,1,0:T(8,128)(2,1)} %pad_maximum_fusion.2), calls=%async_computation.1 | async-start | bytes 786432 | tf_op jit(solution)/shard_map/all_to_all | solution.py:218
  140.7 26.4 %copy-start.22 = (f32[512]{0:T(512)S(1)}, f32[512]{0:T(512)}, u32[]{:S(2)}) copy-start(f32[512]{0:T(512)} %param.29) | copy-start | bytes 6148
  140.7 27.3 %copy-start.34 = (pred[256]{0:T(512)(128)(4,1)S(1)}, pred[256]{0:T(512)(128)(4,1)}, u32[]{:S(2)}) copy-start(pred[256]{0:T(512)(128)(4,1)} %copy-done.33) | copy-start | bytes 772
  (31 other events, 158.2 us)
